TPU v7x, 32 devices: a whole 2x2x4 slice. The times are simulated.
32 devices in a mesh: prow: 4 (over x, core), pcol: 8 (over z, y).
Axes of the slice: x: 2, y: 2, z: 4, core: 2. Of those that a mesh axis runs over, the one named last changes fastest.
Arguments:
- inverse_blocks: bfloat16 [7168, 7168], P('prow', 'pcol'), may hold values from -6 to 6
- lower_late: bfloat16 [56, 128, 256], P('prow', 'pcol'), may hold values from -0.09375 to 0.09375
- lower_early: bfloat16 [56, 128, 256], P('prow', 'pcol'), may hold values from -0.09375 to 0.09375
- link_block: bfloat16 [256, 256], replicated, may hold values from -0.375 to 0.375
- diag_inverse: float32 [2, 256, 256], replicated, may hold values from -6 to 6
- structures: int32 [2, 28], replicated, may hold values from 0 to 55, as said below
Outputs:
- panel_late: float32 [56, 128, 256], P('prow', 'pcol')
- diag_late: float32 [256, 256], replicated
- panel_early: float32 [56, 128, 256], P('prow', 'pcol')
- cross_block: float32 [256, 256], replicated
- diag_early: float32 [256, 256], replicated
Inputs may be any that keep to these rules, and one draw needn't show every extreme that they name: `structures`: each row lists 28 different block numbers in increasing order. Among the 14 blocks with the same value of n // 14 at most 10 are listed, and in each row some such group has exactly 10.
All inputs are finite; a program needn't handle non-finite values.
Results may differ from a plain program's by a relative error of at most 0.01.
Values may be sent and summed in bfloat16 or wider, within the bound.
A program may use at most 64 MiB of HBM per device.

v0:
```python
import jax
import jax.numpy as jnp
from jax import lax
from jax.sharding import PartitionSpec as P

WIDTH = 256
BLK = 128


def from_root(value, axis, source):
    kept = jnp.where(lax.axis_index(axis) == source, value, 0).astype(value.dtype)
    return lax.psum(kept, axis)


def split_parts(values):
    upper = values.astype(jnp.bfloat16)
    lower = (values - upper.astype(jnp.float32)).astype(jnp.bfloat16)
    return (upper, lower)


def rows_product(left, right_float):
    upper, lower = split_parts(right_float)
    dims = (((0,), (0,)), ((), ()))
    first = lax.dot_general(left, upper, dims, preferred_element_type=jnp.float32)
    return first + lax.dot_general(left, lower, dims, preferred_element_type=jnp.float32)


def shards(inverse_blocks, lower_late, lower_early, link_block, diag_inverse, structures):
    high = lax.Precision.HIGHEST
    row_blocks = inverse_blocks.shape[0] // BLK
    col_blocks = inverse_blocks.shape[1] // BLK
    row_id = lax.axis_index("prow")
    col_id = lax.axis_index("pcol")
    block_ids = row_id * row_blocks + jnp.arange(row_blocks, dtype=jnp.int32)

    def block_hits(listed):
        return jnp.any(listed[:, None] == block_ids[None, :], axis=0).astype(jnp.float32)

    def own_columns(strip):
        return lax.dynamic_slice_in_dim(strip, col_id % 2 * col_blocks, col_blocks, 0)

    def reduce_columns(columns, flag_list):
        count = len(flag_list)
        product = jnp.dot(inverse_blocks, columns, preferred_element_type=jnp.float32)
        summed = lax.psum_scatter(
            product.reshape(row_blocks, BLK, count * WIDTH).astype(jnp.bfloat16),
            "pcol",
            scatter_dimension=1,
            tiled=True,
        ).astype(jnp.float32)
        return [summed]

    def separate_reduce(masked, hit_flags):
        strip = lax.all_gather(masked, "pcol", axis=1, tiled=True)
        columns = from_root(own_columns(strip), "prow", col_id // 2)
        columns = columns.reshape(col_blocks * BLK, WIDTH)
        return reduce_columns(columns, [hit_flags])[0]

    hits_late = block_hits(structures[0])
    hits_early = block_hits(structures[1])
    masked_late = lower_late * hits_late.astype(jnp.bfloat16)[:, None, None]
    masked_early = lower_early * hits_early.astype(jnp.bfloat16)[:, None, None]
    late_rows = masked_late.reshape(-1, WIDTH)
    early_rows = masked_early.reshape(-1, WIDTH)
    link_float = link_block.astype(jnp.float32)
    reduced_late = separate_reduce(masked_late, hits_late)
    reduced_early = separate_reduce(masked_early, hits_early)
    panel_late = -(reduced_late * hits_late[:, None, None])
    late_flat = panel_late.reshape(-1, WIDTH)
    local_late = rows_product(late_rows, late_flat)
    cross_local = rows_product(early_rows, late_flat).T
    sum_late = lax.psum(local_late, ("prow", "pcol"))
    diag_late = diag_inverse[0] - sum_late
    flat_upper, flat_lower = split_parts(late_flat)
    carried = jnp.dot(flat_upper, link_block, preferred_element_type=jnp.float32) + jnp.dot(
        flat_lower, link_block, preferred_element_type=jnp.float32
    )
    panel_early = -(
        (reduced_early + carried.reshape(reduced_early.shape)) * hits_early[:, None, None]
    )
    local_early = rows_product(early_rows, panel_early.reshape(-1, WIDTH))
    sum_early, cross_sum = lax.psum((local_early, cross_local), ("prow", "pcol"))
    cross_block = -cross_sum - jnp.dot(diag_late, link_float, precision=high)
    diag_early = diag_inverse[1] - sum_early - jnp.dot(link_float.T, cross_block, precision=high)
    return (panel_late, diag_late, panel_early, cross_block, diag_early)


def solution(mesh):
    placed = (P("prow", "pcol"), P("prow", "pcol", None), P("prow", "pcol", None), P(), P(), P())
    return jax.shard_map(
        shards,
        mesh=mesh,
        in_specs=placed,
        out_specs=(P("prow", "pcol", None), P(), P("prow", "pcol", None), P(), P()),
        check_vma=False,
    )
```

profile of v0, /device:TPU:0, one launch (start us, length us, event | category | flops | bytes accessed | tf_op | source)
XLA Modules:
  0.0 405.6 jit_solution(15092679226556821970)
XLA Ops:
  7.2 0.0 copy-start
  7.2 0.0 all-reduce.7.cloned.1.call-start
  7.3 0.9 slice_bitcast_fusion.1
  8.1 0.2 compare_reduce_fusion
  8.3 1.0 broadcast_multiply_fusion
  9.3 36.2 %all_gather.7 = bf16[14,128,256]{2,1,0:T(8,128)(2,1)} all-gather(bf16[14,16,256]{2,1,0:T(8,128)(2,1)S(1)} %broadcast_multiply_fusion), channel_id=1, replica_groups=mesh['prow'=4,'pcol'=8] {'pcol'}, dimensions={1}, use_global_device_ids=true | all-gather | bytes 1032192 | tf_op jit(solution)/shard_map/all_gather | solution.py:54
  45.5 1.0 broadcast_multiply_fusion.1
  46.5 0.0 copy-start.6
  46.5 0.7 copy-done.6
  47.1 34.3 %all_gather.6 = bf16[14,128,256]{2,1,0:T(8,128)(2,1)} all-gather(bf16[14,16,256]{2,1,0:T(8,128)(2,1)S(1)} %broadcast_multiply_fusion.1), channel_id=1, replica_groups=mesh['prow'=4,'pcol'=8] {'pcol'}, dimensions={1}, use_global_device_ids=true | all-gather | bytes 1032192 | tf_op jit(solution)/shard_map/all_gather | solution.py:54
  81.5 1.8 dynamic-slice_select_fusion
  83.3 1.8 dynamic-slice_select_fusion.1
  85.1 0.0 all-reduce.7.cloned.1.call-update
  85.2 0.0 reduce-scatter.3.cloned.1.call-start
  85.2 37.1 %all-reduce.7.cloned.1.call-done = (bf16[896,256]{1,0:T(8,128)(2,1)}, bf16[896,256]{1,0:T(8,128)(2,1)}) async-done(((bf16[896,256]{1,0:T(8,128)(2,1)}, bf16[896,256]{1,0:T(8,128)(2,1)}), (bf16[896,256]{1,0:T(8,128)(2,1)}, bf16[896,256]{1,0:T(8,128)(2,1)})) %all-reduce.7.cloned.1.call-update) | async-done | bytes 917520 | tf_op jit(solution)/shard_map/psum | solution.py:12
  122.3 0.0 copy-done
  122.3 3.2 fusion
  125.5 2.2 copy.17
  127.7 0.0 reduce-scatter.3.cloned.1.call-update
  127.7 0.0 reduce-scatter.5.cloned.1.call-start
  127.7 3.1 fusion.1
  130.9 0.0 copy-start.1
  130.9 2.3 copy.18
  133.1 0.0 reduce-scatter.5.cloned.1.call-update
  133.1 0.0 all-reduce.5.cloned.1.call-start
  133.2 59.1 %reduce-scatter.3.cloned.1.call-done = bf16[14,16,256]{2,1,0:T(8,128)(2,1)} async-done(((bf16[14,128,256]{2,1,0:T(8,128)(2,1)}), bf16[14,16,256]{2,1,0:T(8,128)(2,1)}) %reduce-scatter.3.cloned.1.call-update) | async-done | bytes 114704 | tf_op jit(solution)/shard_map/reduce_scatter | solution.py:45
  192.3 1.0 multiply_negate_fusion.1
  193.3 0.0 copy-start.4
  193.3 0.9 convolution_bitcast_fusion.3
  194.2 1.8 convolution_bitcast_fusion.5
  196.1 0.0 copy-done.4
  196.1 0.0 copy-done.1
  196.1 0.2 fusion.13
  196.3 0.9 convolution_add_fusion
  197.2 62.1 %reduce-scatter.5.cloned.1.call-done = bf16[14,16,256]{2,1,0:T(8,128)(2,1)} async-done(((bf16[14,128,256]{2,1,0:T(8,128)(2,1)}), bf16[14,16,256]{2,1,0:T(8,128)(2,1)}) %reduce-scatter.5.cloned.1.call-update) | async-done | bytes 114704 | tf_op jit(solution)/shard_map/reduce_scatter | solution.py:45
  259.3 0.0 copy-start.5
  259.3 0.0 copy-start.10
  259.3 0.0 copy-start.7
  259.3 0.0 copy-start.9
  259.3 1.2 multiply_negate_fusion
  260.5 0.0 copy-start.8
  260.5 0.2 convolution_bitcast_fusion.1
  260.7 0.9 fusion.5
  261.6 0.0 copy-done.5
  261.6 0.0 copy-done.10
  261.6 0.9 fusion.4
  262.6 0.0 copy-done.8
  262.6 0.0 copy-done.7
  262.6 0.0 copy-done.9
  262.6 0.9 fusion.3
  263.5 0.0 all-reduce.5.cloned.1.call-update
  263.5 130.9 %all-reduce.5.cloned.1.call-done = (f32[256,256]{1,0:T(8,128)}, f32[256,256]{1,0:T(8,128)}, f32[256,256]{1,0:T(8,128)}) async-done(((f32[256,256]{1,0:T(8,128)}, f32[256,256]{1,0:T(8,128)}, f32[256,256]{1,0:T(8,128)}), (f32[256,256]{1,0:T(8,128)}, f32[256,256]{1,0:T(8,128)}, f32[256,256]{1,0:T(8,128)})) %all-reduce.5.cloned.1.call-update) | async-done | bytes 786448 | tf_op jit(solution)/shard_map/psum | solution.py:72
  394.5 1.1 bitcast_subtract_fusion.1
  395.6 0.0 copy-start.2
  395.6 1.3 convolution_subtract_fusion
  396.9 0.0 copy-start.3
  396.9 2.1 fusion.2
  399.0 0.0 copy-done.2
  399.1 0.0 copy-done.3
  (3 shorter events, 0.0 us)
Async XLA Ops:
  7.2 115.1 %copy-start = (bf16[1792,896]{1,0:T(8,128)(2,1)S(1)}, bf16[1792,896]{1,0:T(8,128)(2,1)}, u32[]{:S(2)}) copy-start(bf16[1792,896]{1,0:T(8,128)(2,1)} %param.6) | copy-start | bytes 9633796
  7.2 115.1 %all-reduce.7.cloned.1.call-start = ((), (), s32[]{:S(2)}) async-start(), calls=%async_computation.5 | async-start | bytes 1835008 | tf_op jit(solution)/shard_map/psum | solution.py:12
  46.5 0.7 copy-start.6
  85.2 107.1 %reduce-scatter.3.cloned.1.call-start = ((), (), s32[]{:S(2)}) async-start(), calls=%async_computation.2 | async-start | bytes 1032192 | tf_op jit(solution)/shard_map/reduce_scatter | solution.py:45
  127.7 131.6 %reduce-scatter.5.cloned.1.call-start = ((), (), s32[]{:S(2)}) async-start(), calls=%async_computation.3 | async-start | bytes 1032192 | tf_op jit(solution)/shard_map/reduce_scatter | solution.py:45
  130.9 65.2 %copy-start.1 = (bf16[256,256]{1,0:T(8,128)(2,1)S(1)}, bf16[256,256]{1,0:T(8,128)(2,1)}, u32[]{:S(2)}) copy-start(bf16[256,256]{1,0:T(8,128)(2,1)} %param.9) | copy-start | bytes 393220
  133.1 261.4 %all-reduce.5.cloned.1.call-start = ((), (), s32[]{:S(2)}) async-start(), calls=%async_computation.4 | async-start | bytes 1572864 | tf_op jit(solution)/shard_map/psum | solution.py:72
  193.3 2.8 copy-start.4
  259.3 2.4 copy-start.5
  259.3 2.4 copy-start.10
  259.3 3.3 copy-start.7
  259.3 3.3 copy-start.9
  260.5 2.1 copy-start.8
  395.6 3.5 copy-start.2
  396.9 2.2 copy-start.3
Sparse Core Ops, SparseCore 0:
  85.3 36.9 all-reduce.6
  127.8 64.4 reduce-scatter.2
  196.0 63.1 reduce-scatter.4
  265.2 129.2 all-reduce.4
where the time goes:
time: 406 us
  waiting for transfers between devices  289 us (71%)
  blocking collectives  70.5 us (17%)
  matrix products  16.6 us (4%)
  between operations  13.9 us (3%)
  other arithmetic  9.06 us (2%)
  local copies, waits for them, and re-layouts  6.03 us (1%)
    psum x1, waiting for transfers between devices, shards(): sum_late = lax.psum(local_late, ('prow', 'pcol'))  131 us
    reduce_scatter x2, waiting for transfers between devices, reduce_columns(): lax.psum_scatter(product.reshape(row_blocks, BLK, count * WIDTH).astype(j...  121 us
    all_gather x2, blocking collectives, separate_reduce(): strip = lax.all_gather(masked, 'pcol', axis=1, tiled=True)  70.5 us
    psum x1, waiting for transfers between devices, from_root(): return lax.psum(kept, axis)  37.1 us
  transfers between devices with their start and end apart: 4, of which 4 were waited for; matrix products, arithmetic and copies ran while one was open for 3% of the time, Pallas kernels for 0%

commit v1 on v0

--- a/solution.py
+++ b/solution.py
@@ -51,7 +51,22 @@
         return [summed]
 
     def separate_reduce(masked, hit_flags):
-        strip = lax.all_gather(masked, "pcol", axis=1, tiled=True)
+        workers = lax.axis_size("pcol")
+        blocks_here = []
+        for to_i in range(workers):
+            blocks_here.append((to_i, (to_i + 1) % workers))
+        heap = []
+        for to_i in range(workers):
+            heap.append((to_i, (to_i - 1) % workers))
+        x_now, piece_out = ([masked], [masked])
+        for _ in range(workers // 2):
+            f_now = lax.ppermute(x_now[-1], "pcol", blocks_here)
+            x_now.append(f_now)
+        for _ in range((workers - 1) // 2):
+            piece_out.append(lax.ppermute(piece_out[-1], "pcol", heap))
+        carry = jnp.concatenate([*x_now[::-1], *piece_out[1:]], 1)
+        side_arr = lax.axis_index("pcol")
+        strip = jnp.roll(carry, (side_arr - workers // 2) * masked.shape[1], 1)
         columns = from_root(own_columns(strip), "prow", col_id // 2)
         columns = columns.reshape(col_blocks * BLK, WIDTH)
         return reduce_columns(columns, [hit_flags])[0]

time: 406 us -> 379 us (0.933)
  blocking collectives: 70.5 us -> 0 us
  starting transfers between devices: 0.16 us -> 24.9 us
  waiting for transfers between devices: 289 us -> 298 us
  local copies, waits for them, and re-layouts: 6.03 us -> 15 us
    all_gather x2 -> x0, blocking collectives: 70.5 us -> none  [separate_reduce(): strip = lax.all_gather(masked, 'pcol', axis=1, tiled=True)]
    ppermute x0 -> x14, starting transfers between devices: none -> 24.7 us  [the longest x8 13.6 us: separate_reduce(): f_now = lax.ppermute(x_now[-1], 'pcol', blocks_here)]
    ppermute x0 -> x14, waiting for transfers between devices: none -> 12.8 us  [the longest x8 10.4 us: separate_reduce(): f_now = lax.ppermute(x_now[-1], 'pcol', blocks_here)]
    unnamed x22 -> x40, local copies, waits for them, and re-layouts: 0.71 us -> 9.62 us
  transfers between devices with their start and end apart: 4 -> 18, of which waited for: 4 -> 11; matrix products, arithmetic and copies ran while one was open for 3% -> 6% of each run, Pallas kernels for 0% -> 0%
where the time goes in v1:
time: 379 us; the launch traced here: 378 us
  waiting for transfers between devices  298 us (79%)
  starting transfers between devices  24.9 us (7%)
  matrix products  16.5 us (4%)
  local copies, waits for them, and re-layouts  15 us (4%)
  between operations  14 us (4%)
  other arithmetic  9.64 us (3%)
    psum x1, waiting for transfers between devices, shards(): sum_late = lax.psum(local_late, ('prow', 'pcol'))  130 us
    reduce_scatter x2, waiting for transfers between devices, reduce_columns(): lax.psum_scatter(product.reshape(row_blocks, BLK, count * WIDTH).astype(j...  121 us
    psum x1, waiting for transfers between devices, from_root(): return lax.psum(kept, axis)  33.9 us
    ppermute x8, starting transfers between devices, separate_reduce(): f_now = lax.ppermute(x_now[-1], 'pcol', blocks_here)  13.6 us
    ppermute x6, starting transfers between devices, separate_reduce(): piece_out.append(lax.ppermute(piece_out[-1], 'pcol', heap))  11.2 us
    ppermute x8, waiting for transfers between devices, separate_reduce(): f_now = lax.ppermute(x_now[-1], 'pcol', blocks_here)  10.4 us
    unnamed x40, local copies, waits for them, and re-layouts  9.62 us
  transfers between devices with their start and end apart: 18, of which 11 were waited for; matrix products, arithmetic and copies ran while one was open for 6% of the time, Pallas kernels for 0%

profile of v1, /device:TPU:0, one launch (start us, length us, event | category | flops | bytes accessed | tf_op | source)
XLA Modules:
  0.0 378.4 jit_solution(7036703348480872769)
XLA Ops:
  7.2 0.0 all-reduce.7.cloned.1.call-start
  7.2 0.9 slice_bitcast_fusion.1
  8.1 0.2 compare_reduce_fusion
  8.3 1.0 broadcast_multiply_fusion
  9.3 3.0 collective-permute-start.7
  12.3 1.0 broadcast_multiply_fusion.1
  13.3 1.6 collective-permute-start
  14.9 3.9 %collective-permute-done.7 = bf16[14,16,256]{2,1,0:T(8,128)(2,1)S(1)} collective-permute-done((bf16[14,16,256]{2,1,0:T(8,128)(2,1)S(1)}, bf16[14,16,256]{2,1,0:T(8,128)(2,1)S(1)}, u32[]{:S(2)}, u32[]{:S(2)}) %collective-permute-start.7) | collective-permute-done | bytes 114720 | tf_op jit(solution)/shard_map/ppermute | solution.py:63
  18.7 4.7 %collective-permute-start.11 = (bf16[14,16,256]{2,1,0:T(8,128)(2,1)S(1)}, bf16[14,16,256]{2,1,0:T(8,128)(2,1)}, u32[]{:S(2)}, u32[]{:S(2)}) collective-permute-start(bf16[14,16,256]{2,1,0:T(8,128)(2,1)S(1)} %broadcast_multiply_fusion), channel_id=1, source_target_pairs={{0,7},{1,0},{2,1},{3,2},{4,3},{5,4},{6,5},{7,6},{8,15},{9,8},{10,9... | collective-permute-start | bytes 344072 | tf_op jit(solution)/shard_map/ppermute | solution.py:66
  23.4 0.0 collective-permute-start.4
  23.5 2.0 collective-permute-start.1
  25.5 2.5 collective-permute-done.8
  28.0 2.5 collective-permute-start.9
  30.5 2.2 collective-permute-start.12
  32.7 0.5 collective-permute-done.4
  33.2 1.8 collective-permute-start.5
  35.0 0.3 collective-permute-start.2
  35.3 2.4 collective-permute-done.9
  37.6 2.8 collective-permute-start.10
  40.4 0.1 collective-permute-done.12
  40.5 1.9 collective-permute-start.13
  42.4 1.8 collective-permute-done.5
  44.2 0.6 collective-permute-start.6
  44.8 1.5 collective-permute-start.3
  46.2 0.9 constant_dynamic-update-slice_fusion.15
  47.1 0.9 constant_dynamic-update-slice_fusion.14
  48.0 0.9 constant_dynamic-update-slice_fusion.13
  48.9 0.9 constant_dynamic-update-slice_fusion.12
  49.9 1.0 constant_dynamic-update-slice_fusion.11
  50.8 1.6 collective-permute-done.3
  52.5 0.9 constant_dynamic-update-slice_fusion.6
  53.4 0.9 constant_dynamic-update-slice_fusion.5
  54.3 0.9 constant_dynamic-update-slice_fusion.4
  55.2 1.0 constant_dynamic-update-slice_fusion.3
  56.2 0.9 constant_dynamic-update-slice_fusion.10
  57.1 0.9 constant_dynamic-update-slice_fusion.9
  58.0 1.1 fusion.7
  59.2 0.9 constant_dynamic-update-slice_fusion.1
  60.1 1.1 fusion.9
  61.3 0.0 reduce-scatter.3.cloned.1.call-start
  61.3 33.9 %all-reduce.7.cloned.1.call-done = (bf16[896,256]{1,0:T(8,128)(2,1)}, bf16[896,256]{1,0:T(8,128)(2,1)}) async-done(((bf16[896,256]{1,0:T(8,128)(2,1)}, bf16[896,256]{1,0:T(8,128)(2,1)}), (bf16[896,256]{1,0:T(8,128)(2,1)}, bf16[896,256]{1,0:T(8,128)(2,1)})) %all-reduce.7.cloned.1.call-update) | async-done | bytes 917520 | tf_op jit(solution)/shard_map/psum | solution.py:12
  95.2 3.1 fusion
  98.3 2.2 copy.17
  100.6 0.0 reduce-scatter.5.cloned.1.call-start
  100.6 3.1 fusion.1
  103.7 2.3 copy.18
  106.0 0.0 all-reduce.5.cloned.1.call-start
  106.1 59.1 %reduce-scatter.3.cloned.1.call-done = bf16[14,16,256]{2,1,0:T(8,128)(2,1)} async-done(((bf16[14,128,256]{2,1,0:T(8,128)(2,1)}), bf16[14,16,256]{2,1,0:T(8,128)(2,1)}) %reduce-scatter.3.cloned.1.call-update) | async-done | bytes 114704 | tf_op jit(solution)/shard_map/reduce_scatter | solution.py:45
  165.2 1.0 multiply_negate_fusion.1
  166.2 0.9 convolution_bitcast_fusion.3
  167.1 1.8 convolution_bitcast_fusion.5
  169.0 0.2 fusion.17
  169.2 0.9 convolution_add_fusion
  170.1 62.1 %reduce-scatter.5.cloned.1.call-done = bf16[14,16,256]{2,1,0:T(8,128)(2,1)} async-done(((bf16[14,128,256]{2,1,0:T(8,128)(2,1)}), bf16[14,16,256]{2,1,0:T(8,128)(2,1)}) %reduce-scatter.5.cloned.1.call-update) | async-done | bytes 114704 | tf_op jit(solution)/shard_map/reduce_scatter | solution.py:45
  232.2 1.2 multiply_negate_fusion
  233.3 0.2 convolution_bitcast_fusion.1
  233.6 0.4 copy-done.6
  234.0 0.9 fusion.5
  235.0 0.9 fusion.4
  235.9 0.9 fusion.3
  236.9 130.5 %all-reduce.5.cloned.1.call-done = (f32[256,256]{1,0:T(8,128)}, f32[256,256]{1,0:T(8,128)}, f32[256,256]{1,0:T(8,128)}) async-done(((f32[256,256]{1,0:T(8,128)}, f32[256,256]{1,0:T(8,128)}, f32[256,256]{1,0:T(8,128)}), (f32[256,256]{1,0:T(8,128)}, f32[256,256]{1,0:T(8,128)}, f32[256,256]{1,0:T(8,128)})) %all-reduce.5.cloned.1.call-update) | async-done | bytes 786448 | tf_op jit(solution)/shard_map/psum | solution.py:87
  367.3 1.1 bitcast_subtract_fusion.1
  368.4 1.3 convolution_subtract_fusion
  369.8 2.1 fusion.2
  (46 shorter events, 0.2 us)
Async XLA Ops:
  7.2 88.0 %copy-start = (bf16[1792,896]{1,0:T(8,128)(2,1)S(1)}, bf16[1792,896]{1,0:T(8,128)(2,1)}, u32[]{:S(2)}) copy-start(bf16[1792,896]{1,0:T(8,128)(2,1)} %param.8) | copy-start | bytes 9633796
  7.2 88.0 %all-reduce.7.cloned.1.call-start = ((), (), s32[]{:S(2)}) async-start(), calls=%async_computation.5 | async-start | bytes 1835008 | tf_op jit(solution)/shard_map/psum | solution.py:12
  9.3 9.4 %collective-permute-start.7 = (bf16[14,16,256]{2,1,0:T(8,128)(2,1)S(1)}, bf16[14,16,256]{2,1,0:T(8,128)(2,1)S(1)}, u32[]{:S(2)}, u32[]{:S(2)}) collective-permute-start(bf16[14,16,256]{2,1,0:T(8,128)(2,1)S(1)} %broadcast_multiply_fusion), channel_id=1, source_target_pairs={{0,1},{1,2},{2,3},{3,4},{4,5},{5,6},{6,7},{7,0},{8,9},{9,10},{10,1... | collective-permute-start | bytes 344072 | tf_op jit(solution)/shard_map/ppermute | solution.py:63
  13.3 17.2 %copy-start.7 = (bf16[14,16,256]{2,1,0:T(8,128)(2,1)}, bf16[14,16,256]{2,1,0:T(8,128)(2,1)S(1)}, u32[]{:S(2)}) copy-start(bf16[14,16,256]{2,1,0:T(8,128)(2,1)S(1)} %broadcast_multiply_fusion.1) | copy-start | bytes 344068
  13.3 10.2 %collective-permute-start = (bf16[14,16,256]{2,1,0:T(8,128)(2,1)S(1)}, bf16[14,16,256]{2,1,0:T(8,128)(2,1)S(1)}, u32[]{:S(2)}, u32[]{:S(2)}) collective-permute-start(bf16[14,16,256]{2,1,0:T(8,128)(2,1)S(1)} %broadcast_multiply_fusion.1), channel_id=1, source_target_pairs={{0,1},{1,2},{2,3},{3,4},{4,5},{5,6},{6,7},{7,0},{8,9},{9,10},{10,1... | collective-permute-start | bytes 344072 | tf_op jit(solution)/shard_map/ppermute | solution.py:63
  18.7 16.3 %copy-start.10 = (bf16[14,16,256]{2,1,0:T(8,128)(2,1)}, bf16[14,16,256]{2,1,0:T(8,128)(2,1)S(1)}, u32[]{:S(2)}) copy-start(bf16[14,16,256]{2,1,0:T(8,128)(2,1)S(1)} %collective-permute-done.7) | copy-start | bytes 344068
  18.7 9.3 %collective-permute-start.8 = (bf16[14,16,256]{2,1,0:T(8,128)(2,1)S(1)}, bf16[14,16,256]{2,1,0:T(8,128)(2,1)S(1)}, u32[]{:S(2)}, u32[]{:S(2)}) collective-permute-start(bf16[14,16,256]{2,1,0:T(8,128)(2,1)S(1)} %collective-permute-done.7), channel_id=1, source_target_pairs={{0,1},{1,2},{2,3},{3,4},{4,5},{5,6},{6,7},{7,0},{8,9},{9,10},{10,1... | collective-permute-start | bytes 344072 | tf_op jit(solution)/shard_map/ppermute | solution.py:63
  18.7 11.7 %collective-permute-start.11 = (bf16[14,16,256]{2,1,0:T(8,128)(2,1)S(1)}, bf16[14,16,256]{2,1,0:T(8,128)(2,1)}, u32[]{:S(2)}, u32[]{:S(2)}) collective-permute-start(bf16[14,16,256]{2,1,0:T(8,128)(2,1)S(1)} %broadcast_multiply_fusion), channel_id=1, source_target_pairs={{0,7},{1,0},{2,1},{3,2},{4,3},{5,4},{6,5},{7,6},{8,15},{9,8},{10,9... | collective-permute-start | bytes 344072 | tf_op jit(solution)/shard_map/ppermute | solution.py:66
  23.4 9.8 %collective-permute-start.4 = (bf16[14,16,256]{2,1,0:T(8,128)(2,1)S(1)}, bf16[14,16,256]{2,1,0:T(8,128)(2,1)S(1)}, u32[]{:S(2)}, u32[]{:S(2)}) collective-permute-start(bf16[14,16,256]{2,1,0:T(8,128)(2,1)S(1)} %broadcast_multiply_fusion.1), channel_id=1, source_target_pairs={{0,7},{1,0},{2,1},{3,2},{4,3},{5,4},{6,5},{7,6},{8,15},{9,8},{10,9... | collective-permute-start | bytes 344072 | tf_op jit(solution)/shard_map/ppermute | solution.py:66
  23.5 9.7 %copy-start.9 = (bf16[14,16,256]{2,1,0:T(8,128)(2,1)}, bf16[14,16,256]{2,1,0:T(8,128)(2,1)S(1)}, u32[]{:S(2)}) copy-start(bf16[14,16,256]{2,1,0:T(8,128)(2,1)S(1)} %collective-permute-done) | copy-start | bytes 344068
  23.5 11.5 %collective-permute-start.1 = (bf16[14,16,256]{2,1,0:T(8,128)(2,1)S(1)}, bf16[14,16,256]{2,1,0:T(8,128)(2,1)}, u32[]{:S(2)}, u32[]{:S(2)}) collective-permute-start(bf16[14,16,256]{2,1,0:T(8,128)(2,1)S(1)} %collective-permute-done), channel_id=1, source_target_pairs={{0,1},{1,2},{2,3},{3,4},{4,5},{5,6},{6,7},{7,0},{8,9},{9,10},{10,1... | collective-permute-start | bytes 344072 | tf_op jit(solution)/shard_map/ppermute | solution.py:63
  28.0 7.3 %copy-start.11 = (bf16[14,16,256]{2,1,0:T(8,128)(2,1)}, bf16[14,16,256]{2,1,0:T(8,128)(2,1)S(1)}, u32[]{:S(2)}) copy-start(bf16[14,16,256]{2,1,0:T(8,128)(2,1)S(1)} %collective-permute-done.8) | copy-start | bytes 344068
  28.0 9.7 %collective-permute-start.9 = (bf16[14,16,256]{2,1,0:T(8,128)(2,1)S(1)}, bf16[14,16,256]{2,1,0:T(8,128)(2,1)}, u32[]{:S(2)}, u32[]{:S(2)}) collective-permute-start(bf16[14,16,256]{2,1,0:T(8,128)(2,1)S(1)} %collective-permute-done.8), channel_id=1, source_target_pairs={{0,1},{1,2},{2,3},{3,4},{4,5},{5,6},{6,7},{7,0},{8,9},{9,10},{10,1... | collective-permute-start | bytes 344072 | tf_op jit(solution)/shard_map/ppermute | solution.py:63
  30.5 10.0 %collective-permute-start.12 = (bf16[14,16,256]{2,1,0:T(8,128)(2,1)}, bf16[14,16,256]{2,1,0:T(8,128)(2,1)}, u32[]{:S(2)}, u32[]{:S(2)}) collective-permute-start(bf16[14,16,256]{2,1,0:T(8,128)(2,1)} %collective-permute-done.11), channel_id=1, source_target_pairs={{0,7},{1,0},{2,1},{3,2},{4,3},{5,4},{6,5},{7,6},{8,15},{9,8},{10,9... | collective-permute-start | bytes 344072 | tf_op jit(solution)/shard_map/ppermute | solution.py:66
  33.2 11.0 %collective-permute-start.5 = (bf16[14,16,256]{2,1,0:T(8,128)(2,1)S(1)}, bf16[14,16,256]{2,1,0:T(8,128)(2,1)}, u32[]{:S(2)}, u32[]{:S(2)}) collective-permute-start(bf16[14,16,256]{2,1,0:T(8,128)(2,1)S(1)} %collective-permute-done.4), channel_id=1, source_target_pairs={{0,7},{1,0},{2,1},{3,2},{4,3},{5,4},{6,5},{7,6},{8,15},{9,8},{10,9... | collective-permute-start | bytes 344072 | tf_op jit(solution)/shard_map/ppermute | solution.py:66
  35.0 9.8 %collective-permute-start.2 = (bf16[14,16,256]{2,1,0:T(8,128)(2,1)}, bf16[14,16,256]{2,1,0:T(8,128)(2,1)}, u32[]{:S(2)}, u32[]{:S(2)}) collective-permute-start(bf16[14,16,256]{2,1,0:T(8,128)(2,1)} %collective-permute-done.1), channel_id=1, source_target_pairs={{0,1},{1,2},{2,3},{3,4},{4,5},{5,6},{6,7},{7,0},{8,9},{9,10},{10,1... | collective-permute-start | bytes 344072 | tf_op jit(solution)/shard_map/ppermute | solution.py:63
  37.6 8.6 %collective-permute-start.10 = (bf16[14,16,256]{2,1,0:T(8,128)(2,1)}, bf16[14,16,256]{2,1,0:T(8,128)(2,1)}, u32[]{:S(2)}, u32[]{:S(2)}) collective-permute-start(bf16[14,16,256]{2,1,0:T(8,128)(2,1)} %collective-permute-done.9), channel_id=1, source_target_pairs={{0,1},{1,2},{2,3},{3,4},{4,5},{5,6},{6,7},{7,0},{8,9},{9,10},{10,1... | collective-permute-start | bytes 344072 | tf_op jit(solution)/shard_map/ppermute | solution.py:63
  40.5 17.5 %collective-permute-start.13 = (bf16[14,16,256]{2,1,0:T(8,128)(2,1)}, bf16[14,16,256]{2,1,0:T(8,128)(2,1)S(1)}, u32[]{:S(2)}, u32[]{:S(2)}) collective-permute-start(bf16[14,16,256]{2,1,0:T(8,128)(2,1)} %collective-permute-done.12), channel_id=1, source_target_pairs={{0,7},{1,0},{2,1},{3,2},{4,3},{5,4},{6,5},{7,6},{8,15},{9,8},{10,9... | collective-permute-start | bytes 344072 | tf_op jit(solution)/shard_map/ppermute | solution.py:66
  44.2 15.9 %collective-permute-start.6 = (bf16[14,16,256]{2,1,0:T(8,128)(2,1)}, bf16[14,16,256]{2,1,0:T(8,128)(2,1)S(1)}, u32[]{:S(2)}, u32[]{:S(2)}) collective-permute-start(bf16[14,16,256]{2,1,0:T(8,128)(2,1)} %collective-permute-done.5), channel_id=1, source_target_pairs={{0,7},{1,0},{2,1},{3,2},{4,3},{5,4},{6,5},{7,6},{8,15},{9,8},{10,9... | collective-permute-start | bytes 344072 | tf_op jit(solution)/shard_map/ppermute | solution.py:66
  44.8 7.7 %collective-permute-start.3 = (bf16[14,16,256]{2,1,0:T(8,128)(2,1)}, bf16[14,16,256]{2,1,0:T(8,128)(2,1)S(1)}, u32[]{:S(2)}, u32[]{:S(2)}) collective-permute-start(bf16[14,16,256]{2,1,0:T(8,128)(2,1)} %collective-permute-done.2), channel_id=1, source_target_pairs={{0,1},{1,2},{2,3},{3,4},{4,5},{5,6},{6,7},{7,0},{8,9},{9,10},{10,1... | collective-permute-start | bytes 344072 | tf_op jit(solution)/shard_map/ppermute | solution.py:63
  61.3 103.9 %reduce-scatter.3.cloned.1.call-start = ((), (), s32[]{:S(2)}) async-start(), calls=%async_computation.2 | async-start | bytes 1032192 | tf_op jit(solution)/shard_map/reduce_scatter | solution.py:45
  100.6 131.6 %reduce-scatter.5.cloned.1.call-start = ((), (), s32[]{:S(2)}) async-start(), calls=%async_computation.3 | async-start | bytes 1032192 | tf_op jit(solution)/shard_map/reduce_scatter | solution.py:45
  103.7 65.3 %copy-start.1 = (bf16[256,256]{1,0:T(8,128)(2,1)S(1)}, bf16[256,256]{1,0:T(8,128)(2,1)}, u32[]{:S(2)}) copy-start(bf16[256,256]{1,0:T(8,128)(2,1)} %param.11) | copy-start | bytes 393220
  106.0 261.3 %all-reduce.5.cloned.1.call-start = ((), (), s32[]{:S(2)}) async-start(), calls=%async_computation.4 | async-start | bytes 1572864 | tf_op jit(solution)/shard_map/psum | solution.py:87
  166.2 2.8 copy-start.4
  232.2 2.8 copy-start.5
  232.2 2.8 copy-start.13
  232.2 3.7 copy-start.8
  232.2 3.7 copy-start.12
  233.3 0.7 copy-start.6
  368.4 3.5 copy-start.2
  369.7 2.2 copy-start.3
Sparse Core Ops, SparseCore 0:
  61.4 33.7 all-reduce.6
  100.7 64.4 reduce-scatter.2
  168.9 63.1 reduce-scatter.4
  238.1 129.1 all-reduce.4
